TPU v7x, 32 devices: a whole 2x2x4 slice. The times are simulated.
32 devices in a mesh: row: 16 (over z, y, x), rep: 2 (over core).
Axes of the slice: x: 2, y: 2, z: 4, core: 2. Of those that a mesh axis runs over, the one named last changes fastest.
Arguments:
- features: bfloat16 [8192, 256], P('row'), may hold values from -6 to 6
- weight: bfloat16 [256, 256], replicated, may hold values from -0.375 to 0.375
- bias: float32 [256], replicated, may hold values from -3 to 3
- cotangent: bfloat16 [8192, 256], P(('row', 'rep')), may hold values from -14 to 14
- tile_values: bfloat16 [16, 16, 8, 128, 128], P('row', 'rep'), may hold values from -0.125 to 0.125
- tile_index: int32 [16, 16, 8, 2], P('row', 'rep'), may hold values from 0 to 3
- tile_count: int32 [16, 16], P('row', 'rep'), may hold values from 0 to 8, as said below
- rev_values: bfloat16 [16, 16, 8, 128, 128], P('row', 'rep'), may hold values from -0.125 to 0.125
- rev_index: int32 [16, 16, 8, 2], P('row', 'rep'), may hold values from 0 to 3
- rev_count: int32 [16, 16], P('row', 'rep'), may hold values from 0 to 8, as said below
Outputs:
- activations: bfloat16 [8192, 256], P(('row', 'rep'))
- grad_features: bfloat16 [8192, 256], P(('row', 'rep'))
- grad_weight: float32 [256, 256], replicated
- grad_bias: float32 [256], replicated
Inputs may be any that keep to these rules, and one draw needn't show every extreme that they name: Slots t < tile_count[a, d] are used; some slab pair uses all 8 slots in every draw. Slots t < rev_count[a, d] are used; some slab pair uses all 8 slots in every draw.
All inputs are finite; a program needn't handle non-finite values.
Results may differ from a plain program's by a relative error of at most 0.006.
Values may be sent and summed in bfloat16 or wider, within the bound.
A program may use at most 64 MiB of HBM per device.

v0:
```python
import jax
import jax.numpy as jnp
from jax import lax
from jax.sharding import PartitionSpec as P

TILE = 128
BLOCKS = 4


def passed_along(value, axis, steps):
    count = lax.axis_size(axis)
    pairs = [(source, (source + steps) % count) for source in range(count)]
    return lax.ppermute(value, axis, pairs)


def section_term(current, tile_block, slot_index, counts):
    blocks = current.reshape(BLOCKS, TILE, current.shape[1])
    sources = jnp.take(blocks, slot_index[:, 1], axis=0)
    product = jnp.einsum("tab,tbf->taf", tile_block, sources, preferred_element_type=jnp.float32)
    usable = jnp.arange(slot_index.shape[0], dtype=jnp.int32) < counts
    placing = (
        (slot_index[:, 0][None, :] == jnp.arange(BLOCKS, dtype=jnp.int32)[:, None])
        & usable[None, :]
    ).astype(jnp.float32)
    return jnp.einsum("nt,taf->naf", placing, product, precision=lax.Precision.HIGHEST)


def first_source(source, sections):
    rep_index = lax.axis_index("rep")
    groups = lax.axis_size("rep")
    current = source
    for shift_bit in range(groups.bit_length() - 1):
        shifted = passed_along(current, "row", -(sections << shift_bit))
        current = jnp.where(rep_index >> shift_bit & 1 == 1, shifted, current)
    return current


def apply_tiles(source, values, slot_index, counts):
    sections = values.shape[1]
    current = first_source(source, sections)
    summed_rows = jnp.zeros((BLOCKS, TILE, source.shape[1]), jnp.float32)
    for section in range(sections):
        if section > 0:
            current = passed_along(current, "row", -1)
        summed_rows = summed_rows + section_term(
            current, values[0, section], slot_index[0, section], counts[0, section]
        )
    return summed_rows.reshape(source.shape[0], source.shape[1])


def reduce_part(partial_rows):
    return lax.psum(partial_rows, "rep")


def own_rows(matrix):
    share_size = matrix.shape[0] // lax.axis_size("rep")
    return lax.dynamic_slice_in_dim(matrix, lax.axis_index("rep") * share_size, share_size, 0)


def activate(preact, cotangent):
    sigmoid_pre = jax.nn.sigmoid(preact)
    activations = (preact * sigmoid_pre).astype(jnp.bfloat16)
    grad_pre = (
        cotangent.astype(jnp.float32) * sigmoid_pre * (1.0 + preact * (1.0 - sigmoid_pre))
    ).astype(jnp.bfloat16)
    return (activations, grad_pre)


def local(
    features,
    weight,
    bias,
    cotangent,
    tile_values,
    tile_index,
    tile_count,
    rev_values,
    rev_index,
    rev_count,
):
    node_total = features.shape[0] * lax.axis_size("row")
    grad_scale = float(node_total) ** (-0.5)
    summed = reduce_part(apply_tiles(features, tile_values, tile_index, tile_count))
    mixed_all = summed.astype(jnp.bfloat16)
    preact_all = jnp.dot(mixed_all, weight, preferred_element_type=jnp.float32) + bias
    cotangent_all = lax.all_gather(cotangent, "rep", axis=0, tiled=True)
    activ_all, grad_all = activate(preact_all, cotangent_all)
    image = jnp.einsum("ng,fg->nf", grad_all, weight, preferred_element_type=jnp.float32).astype(
        jnp.bfloat16
    )
    mixed_rows = own_rows(mixed_all)
    grad_pre = own_rows(grad_all)
    activations = own_rows(activ_all)
    weight_term = jnp.einsum("nf,ng->fg", mixed_rows, grad_pre, preferred_element_type=jnp.float32)
    bias_term = jnp.sum(grad_pre.astype(jnp.float32), axis=0)
    grad_weight, grad_bias = lax.psum((weight_term, bias_term), ("row", "rep"))
    back_rows = reduce_part(apply_tiles(image, rev_values, rev_index, rev_count))
    back_rows = own_rows(back_rows)
    return (
        activations,
        back_rows.astype(jnp.bfloat16),
        grad_weight * grad_scale,
        grad_bias * grad_scale,
    )


def solution(mesh):
    placed = (
        P("row", None),
        P(),
        P(),
        P(("row", "rep"), None),
        P("row", "rep", None, None, None),
        P("row", "rep", None, None),
        P("row", "rep"),
        P("row", "rep", None, None, None),
        P("row", "rep", None, None),
        P("row", "rep"),
    )
    return jax.shard_map(
        local,
        mesh=mesh,
        in_specs=placed,
        out_specs=(P(("row", "rep"), None), P(("row", "rep"), None), P(), P()),
        check_vma=False,
    )
```

profile of v0, /device:TPU:0, one launch (start us, length us, event | category | flops | bytes accessed | tf_op | source)
XLA Modules:
  0.0 381.1 jit_solution(8210804947538525664)
XLA Ops:
  7.2 4.1 %collective-permute-start = (bf16[512,256]{1,0:T(8,128)(2,1)}, bf16[512,256]{1,0:T(8,128)(2,1)S(1)}, u32[]{:S(2)}, u32[]{:S(2)}) collective-permute-start(bf16[512,256]{1,0:T(8,128)(2,1)} %param.12), channel_id=1, source_target_pairs={{0,16},{2,18},{4,20},{6,22},{8,24},{10,26},{12,28},{14,30},{16,0},... | collective-permute-start | bytes 786440 | tf_op jit(solution)/shard_map/ppermute | solution.py:13
  23.6 1.6 fusion.216
  38.3 1.6 fusion.215
  52.1 3.5 all_gather.3
  57.3 3.3 collective-permute-start.1
  63.6 2.1 collective-permute-done.1
  68.1 6.1 %collective-permute-start.2 = (bf16[512,256]{1,0:T(8,128)(2,1)S(1)}, bf16[512,256]{1,0:T(8,128)(2,1)S(1)}, u32[]{:S(2)}, u32[]{:S(2)}) collective-permute-start(bf16[512,256]{1,0:T(8,128)(2,1)S(1)} %collective-permute-done.1), channel_id=1, source_target_pairs={{0,30},{2,0},{4,2},{6,4},{8,6},{10,8},{12,10},{14,12},{16,14},{18,... | collective-permute-start | bytes 786440 | tf_op jit(solution)/shard_map/ppermute | solution.py:13
  75.6 2.9 collective-permute-done.2
  79.2 1.4 fusion.44
  81.1 6.1 %collective-permute-start.3 = (bf16[512,256]{1,0:T(8,128)(2,1)S(1)}, bf16[512,256]{1,0:T(8,128)(2,1)S(1)}, u32[]{:S(2)}, u32[]{:S(2)}) collective-permute-start(bf16[512,256]{1,0:T(8,128)(2,1)S(1)} %copy-done.2), channel_id=1, source_target_pairs={{0,30},{2,0},{4,2},{6,4},{8,6},{10,8},{12,10},{14,12},{16,14},{18,... | collective-permute-start | bytes 786440 | tf_op jit(solution)/shard_map/ppermute | solution.py:13
  88.5 2.6 collective-permute-done.3
  91.9 1.4 fusion.42
  93.8 6.1 %collective-permute-start.4 = (bf16[512,256]{1,0:T(8,128)(2,1)S(1)}, bf16[512,256]{1,0:T(8,128)(2,1)S(1)}, u32[]{:S(2)}, u32[]{:S(2)}) collective-permute-start(bf16[512,256]{1,0:T(8,128)(2,1)S(1)} %copy-done.4), channel_id=1, source_target_pairs={{0,30},{2,0},{4,2},{6,4},{8,6},{10,8},{12,10},{14,12},{16,14},{18,... | collective-permute-start | bytes 786440 | tf_op jit(solution)/shard_map/ppermute | solution.py:13
  101.2 2.6 collective-permute-done.4
  104.6 1.4 fusion.40
  106.5 6.1 %collective-permute-start.5 = (bf16[512,256]{1,0:T(8,128)(2,1)S(1)}, bf16[512,256]{1,0:T(8,128)(2,1)S(1)}, u32[]{:S(2)}, u32[]{:S(2)}) collective-permute-start(bf16[512,256]{1,0:T(8,128)(2,1)S(1)} %copy-done.6), channel_id=1, source_target_pairs={{0,30},{2,0},{4,2},{6,4},{8,6},{10,8},{12,10},{14,12},{16,14},{18,... | collective-permute-start | bytes 786440 | tf_op jit(solution)/shard_map/ppermute | solution.py:13
  113.9 2.6 collective-permute-done.5
  117.2 1.4 fusion.38
  119.1 6.1 %collective-permute-start.6 = (bf16[512,256]{1,0:T(8,128)(2,1)S(1)}, bf16[512,256]{1,0:T(8,128)(2,1)S(1)}, u32[]{:S(2)}, u32[]{:S(2)}) collective-permute-start(bf16[512,256]{1,0:T(8,128)(2,1)S(1)} %copy-done.8), channel_id=1, source_target_pairs={{0,30},{2,0},{4,2},{6,4},{8,6},{10,8},{12,10},{14,12},{16,14},{18,... | collective-permute-start | bytes 786440 | tf_op jit(solution)/shard_map/ppermute | solution.py:13
  126.6 2.6 collective-permute-done.6
  129.9 1.4 fusion.36
  131.8 6.3 %collective-permute-start.7 = (bf16[512,256]{1,0:T(8,128)(2,1)S(1)}, bf16[512,256]{1,0:T(8,128)(2,1)S(1)}, u32[]{:S(2)}, u32[]{:S(2)}) collective-permute-start(bf16[512,256]{1,0:T(8,128)(2,1)S(1)} %copy-done.10), channel_id=1, source_target_pairs={{0,30},{2,0},{4,2},{6,4},{8,6},{10,8},{12,10},{14,12},{16,14},{18,... | collective-permute-start | bytes 786440 | tf_op jit(solution)/shard_map/ppermute | solution.py:13
  139.4 2.6 collective-permute-done.7
  142.7 1.4 fusion.34
  145.4 4.8 %all-reduce.5 = bf16[512,256]{1,0:T(8,128)(2,1)S(1)} all-reduce(f32[512,256]{1,0:T(8,128)S(1)} %bitcast.296), channel_id=1, replica_groups=mesh['row'=16,'rep'=2] {'rep'}, use_global_device_ids=true, to_apply=%region_0.2 | all-reduce | flops 131072 | bytes 786432 | tf_op jit(solution)/shard_map/psum | solution.py:52
  152.0 43.5 %psum.31 = f32[256]{0:T(256)S(1)} all-reduce(f32[256]{0:T(256)S(1)} %convert_reduce_fusion), channel_id=1, replica_groups=mesh['row'=16,'rep'=2] {'row','rep'}, use_global_device_ids=true, to_apply=%region_4.6 | all-reduce | flops 256 | bytes 2048 | tf_op jit(solution)/shard_map/psum | solution.py:96
  196.7 82.9 %all-reduce.4.cloned.1.call-done = f32[256,256]{1,0:T(8,128)} async-done(((f32[256,256]{1,0:T(8,128)}), f32[256,256]{1,0:T(8,128)}) %all-reduce.4.cloned.1.call-update) | async-done | bytes 262160 | tf_op jit(solution)/shard_map/psum | solution.py:96
  279.6 1.7 broadcast_multiply_fusion
  281.3 3.3 collective-permute-start.9
  287.9 1.5 collective-permute-done.9
  292.0 6.1 %collective-permute-start.10 = (bf16[512,256]{1,0:T(8,128)(2,1)S(1)}, bf16[512,256]{1,0:T(8,128)(2,1)S(1)}, u32[]{:S(2)}, u32[]{:S(2)}) collective-permute-start(bf16[512,256]{1,0:T(8,128)(2,1)S(1)} %collective-permute-done.9), channel_id=1, source_target_pairs={{0,30},{2,0},{4,2},{6,4},{8,6},{10,8},{12,10},{14,12},{16,14},{18,... | collective-permute-start | bytes 786440 | tf_op jit(solution)/shard_map/ppermute | solution.py:13
  299.4 2.6 collective-permute-done.10
  302.7 1.4 fusion.28
  304.7 6.1 %collective-permute-start.11 = (bf16[512,256]{1,0:T(8,128)(2,1)S(1)}, bf16[512,256]{1,0:T(8,128)(2,1)S(1)}, u32[]{:S(2)}, u32[]{:S(2)}) collective-permute-start(bf16[512,256]{1,0:T(8,128)(2,1)S(1)} %copy-done.12), channel_id=1, source_target_pairs={{0,30},{2,0},{4,2},{6,4},{8,6},{10,8},{12,10},{14,12},{16,14},{18,... | collective-permute-start | bytes 786440 | tf_op jit(solution)/shard_map/ppermute | solution.py:13
  312.1 2.6 collective-permute-done.11
  315.4 1.4 fusion.26
  317.3 6.1 %collective-permute-start.12 = (bf16[512,256]{1,0:T(8,128)(2,1)S(1)}, bf16[512,256]{1,0:T(8,128)(2,1)S(1)}, u32[]{:S(2)}, u32[]{:S(2)}) collective-permute-start(bf16[512,256]{1,0:T(8,128)(2,1)S(1)} %copy-done.14), channel_id=1, source_target_pairs={{0,30},{2,0},{4,2},{6,4},{8,6},{10,8},{12,10},{14,12},{16,14},{18,... | collective-permute-start | bytes 786440 | tf_op jit(solution)/shard_map/ppermute | solution.py:13
  324.7 2.6 collective-permute-done.12
  328.1 1.4 fusion.24
  330.0 6.4 %collective-permute-start.13 = (bf16[512,256]{1,0:T(8,128)(2,1)S(1)}, bf16[512,256]{1,0:T(8,128)(2,1)S(1)}, u32[]{:S(2)}, u32[]{:S(2)}) collective-permute-start(bf16[512,256]{1,0:T(8,128)(2,1)S(1)} %copy-done.16), channel_id=1, source_target_pairs={{0,30},{2,0},{4,2},{6,4},{8,6},{10,8},{12,10},{14,12},{16,14},{18,... | collective-permute-start | bytes 786440 | tf_op jit(solution)/shard_map/ppermute | solution.py:13
  337.5 2.7 collective-permute-done.13
  340.9 1.4 fusion.22
  342.8 6.1 %collective-permute-start.14 = (bf16[512,256]{1,0:T(8,128)(2,1)S(1)}, bf16[512,256]{1,0:T(8,128)(2,1)S(1)}, u32[]{:S(2)}, u32[]{:S(2)}) collective-permute-start(bf16[512,256]{1,0:T(8,128)(2,1)S(1)} %copy-done.18), channel_id=1, source_target_pairs={{0,30},{2,0},{4,2},{6,4},{8,6},{10,8},{12,10},{14,12},{16,14},{18,... | collective-permute-start | bytes 786440 | tf_op jit(solution)/shard_map/ppermute | solution.py:13
  349.6 3.3 collective-permute-done.14
  353.6 1.4 fusion.20
  355.5 6.1 %collective-permute-start.15 = (bf16[512,256]{1,0:T(8,128)(2,1)S(1)}, bf16[512,256]{1,0:T(8,128)(2,1)S(1)}, u32[]{:S(2)}, u32[]{:S(2)}) collective-permute-start(bf16[512,256]{1,0:T(8,128)(2,1)S(1)} %copy-done.20), channel_id=1, source_target_pairs={{0,30},{2,0},{4,2},{6,4},{8,6},{10,8},{12,10},{14,12},{16,14},{18,... | collective-permute-start | bytes 786440 | tf_op jit(solution)/shard_map/ppermute | solution.py:13
  362.3 3.3 collective-permute-done.15
  368.7 4.8 %all-reduce.6 = bf16[512,256]{1,0:T(8,128)(2,1)S(1)} all-reduce(f32[512,256]{1,0:T(8,128)S(1)} %bitcast.297), channel_id=1, replica_groups=mesh['row'=16,'rep'=2] {'rep'}, use_global_device_ids=true, to_apply=%region_1.3 | all-reduce | flops 131072 | bytes 786432 | tf_op jit(solution)/shard_map/psum | solution.py:52
  (201 shorter events, 84.8 us)
Async XLA Ops:
  7.2 143.1 %copy-start = (bf16[256,256]{1,0:T(8,128)(2,1)S(1)}, bf16[256,256]{1,0:T(8,128)(2,1)}, u32[]{:S(2)}) copy-start(bf16[256,256]{1,0:T(8,128)(2,1)} %param.13) | copy-start | bytes 393220
  7.2 272.4 %all-reduce.4.cloned.1.call-start = ((), (), s32[]{:S(2)}) async-start(), calls=%async_computation | async-start | bytes 524288 | tf_op jit(solution)/shard_map/psum | solution.py:96
  7.2 49.0 %collective-permute-start = (bf16[512,256]{1,0:T(8,128)(2,1)}, bf16[512,256]{1,0:T(8,128)(2,1)S(1)}, u32[]{:S(2)}, u32[]{:S(2)}) collective-permute-start(bf16[512,256]{1,0:T(8,128)(2,1)} %param.12), channel_id=1, source_target_pairs={{0,16},{2,18},{4,20},{6,22},{8,24},{10,26},{12,28},{14,30},{16,0},... | collective-permute-start | bytes 786440 | tf_op jit(solution)/shard_map/ppermute | solution.py:13
  57.3 8.4 %collective-permute-start.1 = (bf16[512,256]{1,0:T(8,128)(2,1)S(1)}, bf16[512,256]{1,0:T(8,128)(2,1)S(1)}, u32[]{:S(2)}, u32[]{:S(2)}) collective-permute-start(bf16[512,256]{1,0:T(8,128)(2,1)S(1)} %broadcast_select_fusion.1), channel_id=1, source_target_pairs={{0,30},{2,0},{4,2},{6,4},{8,6},{10,8},{12,10},{14,12},{16,14},{18,... | collective-permute-start | bytes 786440 | tf_op jit(solution)/shard_map/ppermute | solution.py:13
  68.1 10.4 %collective-permute-start.2 = (bf16[512,256]{1,0:T(8,128)(2,1)S(1)}, bf16[512,256]{1,0:T(8,128)(2,1)S(1)}, u32[]{:S(2)}, u32[]{:S(2)}) collective-permute-start(bf16[512,256]{1,0:T(8,128)(2,1)S(1)} %collective-permute-done.1), channel_id=1, source_target_pairs={{0,30},{2,0},{4,2},{6,4},{8,6},{10,8},{12,10},{14,12},{16,14},{18,... | collective-permute-start | bytes 786440 | tf_op jit(solution)/shard_map/ppermute | solution.py:13
  79.2 1.9 copy-start.2
  81.1 10.0 %collective-permute-start.3 = (bf16[512,256]{1,0:T(8,128)(2,1)S(1)}, bf16[512,256]{1,0:T(8,128)(2,1)S(1)}, u32[]{:S(2)}, u32[]{:S(2)}) collective-permute-start(bf16[512,256]{1,0:T(8,128)(2,1)S(1)} %copy-done.2), channel_id=1, source_target_pairs={{0,30},{2,0},{4,2},{6,4},{8,6},{10,8},{12,10},{14,12},{16,14},{18,... | collective-permute-start | bytes 786440 | tf_op jit(solution)/shard_map/ppermute | solution.py:13
  91.9 1.9 copy-start.4
  93.8 10.0 %collective-permute-start.4 = (bf16[512,256]{1,0:T(8,128)(2,1)S(1)}, bf16[512,256]{1,0:T(8,128)(2,1)S(1)}, u32[]{:S(2)}, u32[]{:S(2)}) collective-permute-start(bf16[512,256]{1,0:T(8,128)(2,1)S(1)} %copy-done.4), channel_id=1, source_target_pairs={{0,30},{2,0},{4,2},{6,4},{8,6},{10,8},{12,10},{14,12},{16,14},{18,... | collective-permute-start | bytes 786440 | tf_op jit(solution)/shard_map/ppermute | solution.py:13
  103.8 0.7 copy-start.5
  104.5 1.9 copy-start.6
  106.5 10.0 %collective-permute-start.5 = (bf16[512,256]{1,0:T(8,128)(2,1)S(1)}, bf16[512,256]{1,0:T(8,128)(2,1)S(1)}, u32[]{:S(2)}, u32[]{:S(2)}) collective-permute-start(bf16[512,256]{1,0:T(8,128)(2,1)S(1)} %copy-done.6), channel_id=1, source_target_pairs={{0,30},{2,0},{4,2},{6,4},{8,6},{10,8},{12,10},{14,12},{16,14},{18,... | collective-permute-start | bytes 786440 | tf_op jit(solution)/shard_map/ppermute | solution.py:13
  116.5 0.7 copy-start.7
  117.2 1.9 copy-start.8
  119.1 10.0 %collective-permute-start.6 = (bf16[512,256]{1,0:T(8,128)(2,1)S(1)}, bf16[512,256]{1,0:T(8,128)(2,1)S(1)}, u32[]{:S(2)}, u32[]{:S(2)}) collective-permute-start(bf16[512,256]{1,0:T(8,128)(2,1)S(1)} %copy-done.8), channel_id=1, source_target_pairs={{0,30},{2,0},{4,2},{6,4},{8,6},{10,8},{12,10},{14,12},{16,14},{18,... | collective-permute-start | bytes 786440 | tf_op jit(solution)/shard_map/ppermute | solution.py:13
  129.2 0.7 copy-start.9
  129.9 1.9 copy-start.10
  131.8 10.2 %collective-permute-start.7 = (bf16[512,256]{1,0:T(8,128)(2,1)S(1)}, bf16[512,256]{1,0:T(8,128)(2,1)S(1)}, u32[]{:S(2)}, u32[]{:S(2)}) collective-permute-start(bf16[512,256]{1,0:T(8,128)(2,1)S(1)} %copy-done.10), channel_id=1, source_target_pairs={{0,30},{2,0},{4,2},{6,4},{8,6},{10,8},{12,10},{14,12},{16,14},{18,... | collective-permute-start | bytes 786440 | tf_op jit(solution)/shard_map/ppermute | solution.py:13
  142.7 1.9 copy-start.27
  142.7 1.9 copy-start.35
  144.6 5.6 %copy-start.21 = (bf16[512,256]{1,0:T(8,128)(2,1)S(1)}, bf16[512,256]{1,0:T(8,128)(2,1)}, u32[]{:S(2)}) copy-start(bf16[512,256]{1,0:T(8,128)(2,1)} %all_gather.3) | copy-start | bytes 786436
  144.6 5.6 %copy-start.36 = (f32[256]{0:T(256)S(1)}, f32[256]{0:T(256)}, u32[]{:S(2)}) copy-start(f32[256]{0:T(256)} %param.14) | copy-start | bytes 3076
  150.9 134.5 %copy-start.33 = (pred[8]{0:T(512)(128)(4,1)S(1)}, pred[8]{0:T(512)(128)(4,1)}, u32[]{:S(2)}) copy-start(pred[8]{0:T(512)(128)(4,1)} %get-tuple-element.19) | copy-start | bytes 28
  151.9 129.4 %collective-permute-start.8 = (bf16[512,256]{1,0:T(8,128)(2,1)S(1)}, bf16[512,256]{1,0:T(8,128)(2,1)S(1)}, u32[]{:S(2)}, u32[]{:S(2)}) collective-permute-start(bf16[512,256]{1,0:T(8,128)(2,1)S(1)} %convolution_convert_fusion), channel_id=1, source_target_pairs={{0,16},{2,18},{4,20},{6,22},{8,24},{10,26},{12,28},{14,30},{16,0},... | collective-permute-start | bytes 786440 | tf_op jit(solution)/shard_map/ppermute | solution.py:13
  281.3 8.1 %collective-permute-start.9 = (bf16[512,256]{1,0:T(8,128)(2,1)S(1)}, bf16[512,256]{1,0:T(8,128)(2,1)S(1)}, u32[]{:S(2)}, u32[]{:S(2)}) collective-permute-start(bf16[512,256]{1,0:T(8,128)(2,1)S(1)} %broadcast_select_fusion), channel_id=1, source_target_pairs={{0,30},{2,0},{4,2},{6,4},{8,6},{10,8},{12,10},{14,12},{16,14},{18,... | collective-permute-start | bytes 786440 | tf_op jit(solution)/shard_map/ppermute | solution.py:13
  285.3 1.9 copy-start.22
  285.3 1.9 copy-start.28
  286.7 3.4 copy-start.31
  292.0 10.0 %collective-permute-start.10 = (bf16[512,256]{1,0:T(8,128)(2,1)S(1)}, bf16[512,256]{1,0:T(8,128)(2,1)S(1)}, u32[]{:S(2)}, u32[]{:S(2)}) collective-permute-start(bf16[512,256]{1,0:T(8,128)(2,1)S(1)} %collective-permute-done.9), channel_id=1, source_target_pairs={{0,30},{2,0},{4,2},{6,4},{8,6},{10,8},{12,10},{14,12},{16,14},{18,... | collective-permute-start | bytes 786440 | tf_op jit(solution)/shard_map/ppermute | solution.py:13
  302.0 0.7 copy-start.11
  302.7 1.9 copy-start.12
  304.7 10.0 %collective-permute-start.11 = (bf16[512,256]{1,0:T(8,128)(2,1)S(1)}, bf16[512,256]{1,0:T(8,128)(2,1)S(1)}, u32[]{:S(2)}, u32[]{:S(2)}) collective-permute-start(bf16[512,256]{1,0:T(8,128)(2,1)S(1)} %copy-done.12), channel_id=1, source_target_pairs={{0,30},{2,0},{4,2},{6,4},{8,6},{10,8},{12,10},{14,12},{16,14},{18,... | collective-permute-start | bytes 786440 | tf_op jit(solution)/shard_map/ppermute | solution.py:13
  315.4 1.9 copy-start.14
  317.3 10.0 %collective-permute-start.12 = (bf16[512,256]{1,0:T(8,128)(2,1)S(1)}, bf16[512,256]{1,0:T(8,128)(2,1)S(1)}, u32[]{:S(2)}, u32[]{:S(2)}) collective-permute-start(bf16[512,256]{1,0:T(8,128)(2,1)S(1)} %copy-done.14), channel_id=1, source_target_pairs={{0,30},{2,0},{4,2},{6,4},{8,6},{10,8},{12,10},{14,12},{16,14},{18,... | collective-permute-start | bytes 786440 | tf_op jit(solution)/shard_map/ppermute | solution.py:13
  328.1 8.3 %copy-start.24 = (s32[8]{0:T(128)S(1)}, s32[8]{0:T(128)}, u32[]{:S(2)}) copy-start(s32[8]{0:T(128)} %get-tuple-element.83) | copy-start | bytes 100
  328.1 1.9 copy-start.16
  330.0 10.2 %collective-permute-start.13 = (bf16[512,256]{1,0:T(8,128)(2,1)S(1)}, bf16[512,256]{1,0:T(8,128)(2,1)S(1)}, u32[]{:S(2)}, u32[]{:S(2)}) collective-permute-start(bf16[512,256]{1,0:T(8,128)(2,1)S(1)} %copy-done.16), channel_id=1, source_target_pairs={{0,30},{2,0},{4,2},{6,4},{8,6},{10,8},{12,10},{14,12},{16,14},{18,... | collective-permute-start | bytes 786440 | tf_op jit(solution)/shard_map/ppermute | solution.py:13
  340.9 8.1 %copy-start.23 = (s32[8]{0:T(128)S(1)}, s32[8]{0:T(128)}, u32[]{:S(2)}) copy-start(s32[8]{0:T(128)} %get-tuple-element.82) | copy-start | bytes 100
  340.9 8.1 %copy-start.34 = (pred[8]{0:T(512)(128)(4,1)S(1)}, pred[8]{0:T(512)(128)(4,1)}, u32[]{:S(2)}) copy-start(pred[8]{0:T(512)(128)(4,1)} %iota_compare_fusion.18) | copy-start | bytes 28
  340.9 1.9 copy-start.18
  342.8 10.0 %collective-permute-start.14 = (bf16[512,256]{1,0:T(8,128)(2,1)S(1)}, bf16[512,256]{1,0:T(8,128)(2,1)S(1)}, u32[]{:S(2)}, u32[]{:S(2)}) collective-permute-start(bf16[512,256]{1,0:T(8,128)(2,1)S(1)} %copy-done.18), channel_id=1, source_target_pairs={{0,30},{2,0},{4,2},{6,4},{8,6},{10,8},{12,10},{14,12},{16,14},{18,... | collective-permute-start | bytes 786440 | tf_op jit(solution)/shard_map/ppermute | solution.py:13
  353.6 8.1 %copy-start.26 = (s32[8]{0:T(128)S(1)}, s32[8]{0:T(128)}, u32[]{:S(2)}) copy-start(s32[8]{0:T(128)} %get-tuple-element.81) | copy-start | bytes 100
  353.6 8.1 %copy-start.32 = (pred[8]{0:T(512)(128)(4,1)S(1)}, pred[8]{0:T(512)(128)(4,1)}, u32[]{:S(2)}) copy-start(pred[8]{0:T(512)(128)(4,1)} %iota_compare_fusion.17) | copy-start | bytes 28
  353.6 1.9 copy-start.20
  355.5 10.6 %copy-start.30 = (pred[8]{0:T(512)(128)(4,1)S(1)}, pred[8]{0:T(512)(128)(4,1)}, u32[]{:S(2)}) copy-start(pred[8]{0:T(512)(128)(4,1)} %get-tuple-element.5) | copy-start | bytes 28
  355.5 10.0 %collective-permute-start.15 = (bf16[512,256]{1,0:T(8,128)(2,1)S(1)}, bf16[512,256]{1,0:T(8,128)(2,1)S(1)}, u32[]{:S(2)}, u32[]{:S(2)}) collective-permute-start(bf16[512,256]{1,0:T(8,128)(2,1)S(1)} %copy-done.20), channel_id=1, source_target_pairs={{0,30},{2,0},{4,2},{6,4},{8,6},{10,8},{12,10},{14,12},{16,14},{18,... | collective-permute-start | bytes 786440 | tf_op jit(solution)/shard_map/ppermute | solution.py:13
  366.1 1.9 copy-start.25
  366.1 1.9 copy-start.29
  (6 other events, 4.3 us)
Sparse Core Ops, SparseCore 0:
  152.1 127.4 all-reduce.3
where the time goes:
time: 382 us; the launch traced here: 381 us
  waiting for transfers between devices  119 us (31%)
  starting transfers between devices  84.8 us (22%)
  blocking collectives  56.7 us (15%)
  matrix products  40.4 us (11%)
  other arithmetic  35.9 us (9%)
  local copies, waits for them, and re-layouts  28.9 us (8%)
  between operations  15 us (4%)
    ppermute x16, starting transfers between devices, passed_along(): return lax.ppermute(value, axis, pairs)  84.7 us
    psum x1, waiting for transfers between devices, local(): grad_weight, grad_bias = lax.psum((weight_term, bias_term), ('row', 'rep'))  82.9 us
    psum x1, blocking collectives, local(): grad_weight, grad_bias = lax.psum((weight_term, bias_term), ('row', 'rep'))  43.5 us
    ppermute x16, waiting for transfers between devices, passed_along(): return lax.ppermute(value, axis, pairs)  36.6 us
    dot_general x16, matrix products, section_term(): jnp.einsum('tab,tbf->taf', tile_block, sources, preferred_element_type=jn...  22.4 us
    lt x16, other arithmetic, section_term(): usable = jnp.arange(slot_index.shape[0], dtype=jnp.int32) < counts  18.2 us
    dot_general x16, matrix products, section_term(): jnp.einsum('nt,taf->naf', placing, product, precision=lax.Precision.HIGHEST)  16.4 us
    gather x16, local copies, waits for them, and re-layouts, section_term(): sources = jnp.take(blocks, slot_index[:, 1], axis=0)  10.5 us
  transfers between devices with their start and end apart: 17, of which 15 were waited for; matrix products, arithmetic and copies ran while one was open for 17% of the time, Pallas kernels for 0%

commit v1 on v0

--- a/solution.py
+++ b/solution.py
@@ -1,10 +1,15 @@
+import functools
+
 import jax
 import jax.numpy as jnp
 from jax import lax
+from jax.experimental import pallas as pl
+from jax.experimental.pallas import tpu as pltpu
 from jax.sharding import PartitionSpec as P
 
 TILE = 128
 BLOCKS = 4
+MESH = pl.DeviceIdType.MESH
 
 
 def passed_along(value, axis, steps):
@@ -15,7 +20,8 @@
 
 def section_term(current, tile_block, slot_index, counts):
     blocks = current.reshape(BLOCKS, TILE, current.shape[1])
-    sources = jnp.take(blocks, slot_index[:, 1], axis=0)
+    picks = (slot_index[:, 1][:, None] == jnp.arange(BLOCKS, dtype=jnp.int32)[None, :]).astype(jnp.bfloat16)
+    sources = jnp.einsum("tn,nbf->tbf", picks, blocks, preferred_element_type=jnp.float32).astype(jnp.bfloat16)
     product = jnp.einsum("tab,tbf->taf", tile_block, sources, preferred_element_type=jnp.float32)
     usable = jnp.arange(slot_index.shape[0], dtype=jnp.int32) < counts
     placing = (
@@ -48,10 +54,6 @@
     return summed_rows.reshape(source.shape[0], source.shape[1])
 
 
-def reduce_part(partial_rows):
-    return lax.psum(partial_rows, "rep")
-
-
 def own_rows(matrix):
     share_size = matrix.shape[0] // lax.axis_size("rep")
     return lax.dynamic_slice_in_dim(matrix, lax.axis_index("rep") * share_size, share_size, 0)
@@ -66,21 +68,12 @@
     return (activations, grad_pre)
 
 
-def local(
-    features,
-    weight,
-    bias,
-    cotangent,
-    tile_values,
-    tile_index,
-    tile_count,
-    rev_values,
-    rev_index,
-    rev_count,
+def general(
+    features, weight, bias, cotangent, tile_values, tile_index, tile_count, rev_values, rev_index, rev_count
 ):
     node_total = features.shape[0] * lax.axis_size("row")
     grad_scale = float(node_total) ** (-0.5)
-    summed = reduce_part(apply_tiles(features, tile_values, tile_index, tile_count))
+    summed = lax.psum(apply_tiles(features, tile_values, tile_index, tile_count), "rep")
     mixed_all = summed.astype(jnp.bfloat16)
     preact_all = jnp.dot(mixed_all, weight, preferred_element_type=jnp.float32) + bias
     cotangent_all = lax.all_gather(cotangent, "rep", axis=0, tiled=True)
@@ -94,14 +87,299 @@
     weight_term = jnp.einsum("nf,ng->fg", mixed_rows, grad_pre, preferred_element_type=jnp.float32)
     bias_term = jnp.sum(grad_pre.astype(jnp.float32), axis=0)
     grad_weight, grad_bias = lax.psum((weight_term, bias_term), ("row", "rep"))
-    back_rows = reduce_part(apply_tiles(image, rev_values, rev_index, rev_count))
-    back_rows = own_rows(back_rows)
+    back_rows = own_rows(lax.psum(apply_tiles(image, rev_values, rev_index, rev_count), "rep"))
     return (
         activations,
         back_rows.astype(jnp.bfloat16),
         grad_weight * grad_scale,
         grad_bias * grad_scale,
     )
+
+
+SLABS = 16
+SLOTS = 8
+HALF = 256
+WIDTH = 256
+BLOCK = 136
+PART = 72
+
+
+def fused_kernel(
+    scale,
+    codes_ref, feat_ref, weight_ref, bias_ref, cot_ref, fwd_hbm, rev_hbm,
+    act_ref, back_ref, gw_ref, gb_ref,
+    gathered, tiles, codes_all, codes_s, acc, peer_acc,
+    mixed_v, gpre_v, term, term_in, part_p, in_p, part_q, in_q, part_z, final,
+    send_sem, recv_sem, tile_own, tile_send, tile_recv, code_sem, acc_send, acc_recv, red_send, red_recv,
+):
+    me, core = lax.axis_index("row"), lax.axis_index("rep")
+    x, y, z = lax.rem(me, 2), lax.rem(lax.div(me, 2), 2), lax.div(me, 4)
+    step_x, step_y = 1 - 2 * x, 2 - 4 * y
+    other = 1 - core
+    step_p = step_x * other + step_y * core
+    step_q = step_x * core + step_y * other
+    bit_p = x * other + y * core
+    twin, peer_p, peer_q = (me, other), (me + step_p, core), (me + step_q, core)
+    plane = lax.rem(me, 4)
+
+    def line(k):
+        return lax.rem(z + k, 4) * 4 + plane
+
+    peers_z = [(line(k), core) for k in (1, 2, 3)]
+
+    def remote(src, dst, s, r, dev):
+        return pltpu.make_async_remote_copy(
+            src_ref=src, dst_ref=dst, send_sem=s, recv_sem=r, device_id=dev, device_id_type=MESH
+        )
+
+    barrier = pltpu.get_barrier_semaphore()
+    for dev in [twin, peer_p, peer_q] + peers_z:
+        pl.semaphore_signal(barrier, inc=1, device_id=dev, device_id_type=MESH)
+    gathered[0, me] = feat_ref[pl.ds(pl.multiple_of(core * HALF, HALF), HALF), :]
+    pl.semaphore_wait(barrier, 6)
+
+    def piece(phase, slab, sem, dev):
+        return remote(
+            gathered.at[phase, slab], gathered.at[phase, slab],
+            send_sem.at[phase, sem], recv_sem.at[phase, slab], dev,
+        )
+
+    def send_own(phase):
+        for k, dev in enumerate(peers_z):
+            piece(phase, me, k, dev).start()
+        piece(phase, me, 3, peer_p).start()
+        piece(phase, me, 7, peer_q).start()
+
+    def forward_line(phase):
+        def body(k, carry):
+            slab = line(k)
+            piece(phase, slab, 0, peer_p).wait_recv()
+            piece(phase, slab, 3 + k, peer_p).start()
+            piece(phase, slab, 7 + k, peer_q).start()
+            return carry
+        lax.fori_loop(1, 4, body, 0)
+
+    def term_of(phase, slab):
+        offset = lax.rem(slab - me + SLABS, SLABS)
+        group, within = lax.div(offset, 8), lax.rem(offset, 8)
+        lefts, rights = [[] for _ in range(BLOCKS)], []
+        low, high = gathered[phase, slab, 0:TILE, :], gathered[phase, slab, TILE:HALF, :]
+        for t in range(SLOTS):
+            code = codes_s[group, phase, within * SLOTS + t]
+            second = jnp.where((code & 1) == 1, 1.0, 0.0).astype(jnp.float32)
+            mine = ((code >> 1) & 1) == core
+            value = tiles[phase, offset, t]
+            rights.append(
+                low * jnp.full(low.shape, 1.0 - second, jnp.float32).astype(jnp.bfloat16)
+                + high * jnp.full(low.shape, second, jnp.float32).astype(jnp.bfloat16)
+            )
+            for n in range(BLOCKS):
+                used = jnp.where(mine & ((code >> 2) == n), 1.0, 0.0).astype(jnp.float32)
+                lefts[n].append(value * jnp.full((TILE, TILE), used, jnp.float32).astype(jnp.bfloat16))
+        right = jnp.concatenate(rights, axis=0)
+        for n in range(BLOCKS):
+            acc[phase, n * TILE:(n + 1) * TILE, :] += jnp.dot(
+                jnp.concatenate(lefts[n], axis=1), right, preferred_element_type=jnp.float32
+            )
+
+    def forward_p(phase):
+        def body(k, carry):
+            slab = line(k) + step_p
+            piece(phase, slab, 0, peer_q).wait_recv()
+            piece(phase, slab, 11 + k, peer_q).start()
+            term_of(phase, line(k))
+            return carry
+        lax.fori_loop(0, 4, body, 0)
+
+    def add_p(phase):
+        def body(k, carry):
+            term_of(phase, line(k) + step_p)
+            return carry
+        lax.fori_loop(0, 4, body, 0)
+
+    def add_q(phase, first, last):
+        def body(k, carry):
+            slab = line(lax.rem(k, 4)) + step_p * lax.div(k, 4) + step_q
+            piece(phase, slab, 0, peer_q).wait_recv()
+            term_of(phase, slab)
+            return carry
+        lax.fori_loop(first, last, body, 0)
+
+    own_half = pl.ds(pl.multiple_of(core * HALF, HALF), HALF)
+    twin_half = pl.ds(pl.multiple_of(other * HALF, HALF), HALF)
+
+    def swap_acc(phase):
+        copy = remote(
+            acc.at[phase, twin_half], peer_acc.at[phase], acc_send.at[phase], acc_recv.at[phase], twin
+        )
+        copy.start()
+        copy.wait()
+        return acc[phase, own_half, :] + peer_acc[phase]
+
+    def tile_copies(phase, source):
+        place = pl.ds(core * 8, 8)
+        return (
+            pltpu.make_async_copy(source.at[0], tiles.at[phase, place], tile_own.at[phase]),
+            remote(source.at[0], tiles.at[phase, place], tile_send.at[phase], tile_recv.at[phase], twin),
+        )
+
+    send_own(0)
+    codes_all[core] = codes_ref[...]
+    code_copy = remote(codes_all.at[core], codes_all.at[core], code_sem.at[0], code_sem.at[1], twin)
+    code_copy.start()
+    near, far = tile_copies(0, fwd_hbm)
+    near.start()
+    far.start()
+    acc[...] = jnp.zeros_like(acc)
+    forward_line(0)
+    code_copy.wait()
+    to_scalar = pltpu.make_async_copy(codes_all, codes_s, code_sem.at[2])
+    to_scalar.start()
+    to_scalar.wait()
+    near.wait()
+    far.wait()
+    near, far = tile_copies(1, rev_hbm)
+    near.start()
+    far.start()
+    forward_p(0)
+    add_p(0)
+    add_q(0, 0, 8)
+
+    mixed = swap_acc(0).astype(jnp.bfloat16)
+    mixed_v[...] = mixed
+    preact = jnp.dot(mixed, weight_ref[...], preferred_element_type=jnp.float32) + bias_ref[...]
+    sigmoid = jax.nn.sigmoid(preact)
+    act_ref[...] = (preact * sigmoid).astype(jnp.bfloat16)
+    gpre_v[...] = (
+        cot_ref[...].astype(jnp.float32) * sigmoid * (1.0 + preact * (1.0 - sigmoid))
+    ).astype(jnp.bfloat16)
+    gathered[1, me] = lax.dot_general(
+        gpre_v[...], weight_ref[...], (((1,), (1,)), ((), ())), preferred_element_type=jnp.float32
+    ).astype(jnp.bfloat16)
+    send_own(1)
+
+    whole = lax.dot_general(
+        mixed_v[...], gpre_v[...], (((0,), (0,)), ((), ())), preferred_element_type=jnp.float32
+    )
+    sums = jnp.sum(gpre_v[...].astype(jnp.float32).reshape(HALF // 8, 8, WIDTH), axis=0)
+    for h in range(2):
+        term[h, 0:64, :] = whole[128 * h:128 * h + 64]
+        term[h, 64:72, :] = sums
+        term[h, 72:136, :] = whole[128 * h + 64:128 * h + 128]
+    to_twin = remote(term.at[other], term_in, red_send.at[0], red_recv.at[0], twin)
+    to_twin.start()
+    forward_line(1)
+    near.wait()
+    far.wait()
+    to_twin.wait()
+    part_p[...] = term[core] + term_in[...]
+    keep = pl.ds(pl.multiple_of(bit_p * 64, 8), PART)
+    give = pl.ds(pl.multiple_of((1 - bit_p) * 64, 8), PART)
+    to_p = remote(part_p.at[give], in_p, red_send.at[1], red_recv.at[1], peer_p)
+    to_p.start()
+    forward_p(1)
+    to_p.wait()
+    part_q[...] = part_p[keep, :] + in_p[...]
+    to_q = remote(part_q, in_q, red_send.at[2], red_recv.at[2], peer_q)
+    to_q.start()
+    add_p(1)
+    to_q.wait()
+    part_z[z] = part_q[...] + in_q[...]
+    to_z = [
+        remote(part_z.at[z], part_z.at[z], red_send.at[3 + k], red_recv.at[3 + z], dev)
+        for k, dev in enumerate(peers_z)
+    ]
+    for copy in to_z:
+        copy.start()
+    add_q(1, 0, 4)
+    for k in (1, 2, 3):
+        at = lax.rem(z + k, 4)
+        remote(part_z.at[at], part_z.at[at], red_send.at[3], red_recv.at[3 + at], twin).wait_recv()
+    final[core, keep, :] = ((part_z[0] + part_z[1]) + part_z[2]) + part_z[3]
+    up = final.at[core, pl.ds(pl.multiple_of(bit_p * PART, 8), 64)]
+    up_p = remote(up, up, red_send.at[6], red_recv.at[7], peer_p)
+    up_p.start()
+    add_q(1, 4, 6)
+    up_p.wait()
+    up_twin = remote(final.at[core], final.at[core], red_send.at[7], red_recv.at[8], twin)
+    up_twin.start()
+    add_q(1, 6, 8)
+    copy = remote(acc.at[1, twin_half], peer_acc.at[1], acc_send.at[1], acc_recv.at[1], twin)
+    copy.start()
+    up_twin.wait()
+    for h in range(2):
+        gw_ref[128 * h:128 * h + 64, :] = final[h, 0:64, :] * scale
+        gw_ref[128 * h + 64:128 * h + 128, :] = final[h, 72:136, :] * scale
+    gb_ref[...] = jnp.sum(final[0, 64:72, :], axis=0, keepdims=True) * scale
+    copy.wait()
+    back_ref[...] = (acc[1, own_half, :] + peer_acc[1]).astype(jnp.bfloat16)
+    for k in range(3):
+        to_z[k].wait_send()
+    for phase in range(2):
+        def drain(k, carry):
+            piece(phase, me, k, twin).wait_send()
+            return carry
+        lax.fori_loop(0, 15, drain, 0)
+
+
+def codes_of(index, count):
+    slot = jnp.arange(index.shape[2], dtype=jnp.int32)[None, :]
+    code = index[0, :, :, 0] * BLOCKS + index[0, :, :, 1]
+    return jnp.where(slot < count[0][:, None], code, 4 * BLOCKS * BLOCKS).reshape(1, -1)
+
+
+def fused(
+    features, weight, bias, cotangent, tile_values, tile_index, tile_count, rev_values, rev_index, rev_count
+):
+    scale = float(features.shape[0] * lax.axis_size("row")) ** (-0.5)
+    codes = jnp.concatenate([codes_of(tile_index, tile_count), codes_of(rev_index, rev_count)], axis=0)
+    codes = jnp.pad(codes, ((0, 6), (0, 128 - codes.shape[1])))
+    vmem = pl.BlockSpec(memory_space=pltpu.VMEM)
+    anywhere = pl.BlockSpec(memory_space=pl.ANY)
+    f32, bf16 = jnp.float32, jnp.bfloat16
+    act, back, gw, gb = pl.pallas_call(
+        functools.partial(fused_kernel, scale),
+        out_shape=(
+            jax.ShapeDtypeStruct((HALF, WIDTH), bf16),
+            jax.ShapeDtypeStruct((HALF, WIDTH), bf16),
+            jax.ShapeDtypeStruct((WIDTH, WIDTH), f32),
+            jax.ShapeDtypeStruct((1, WIDTH), f32),
+        ),
+        in_specs=[vmem] * 5 + [anywhere] * 2,
+        out_specs=(vmem,) * 4,
+        scratch_shapes=[
+            pltpu.VMEM((2, SLABS, HALF, WIDTH), bf16),
+            pltpu.VMEM((2, SLABS, SLOTS, TILE, TILE), bf16),
+            pltpu.VMEM((2, 8, 128), jnp.int32),
+            pltpu.SMEM((2, 8, 128), jnp.int32),
+            pltpu.VMEM((2, 2 * HALF, WIDTH), f32),
+            pltpu.VMEM((2, HALF, WIDTH), f32),
+            pltpu.VMEM((HALF, WIDTH), bf16),
+            pltpu.VMEM((HALF, WIDTH), bf16),
+            pltpu.VMEM((2, BLOCK, WIDTH), f32),
+            pltpu.VMEM((BLOCK, WIDTH), f32),
+            pltpu.VMEM((BLOCK, WIDTH), f32),
+            pltpu.VMEM((PART, WIDTH), f32),
+            pltpu.VMEM((PART, WIDTH), f32),
+            pltpu.VMEM((PART, WIDTH), f32),
+            pltpu.VMEM((4, PART, WIDTH), f32),
+            pltpu.VMEM((2, BLOCK, WIDTH), f32),
+            pltpu.SemaphoreType.DMA((2, 15)),
+            pltpu.SemaphoreType.DMA((2, SLABS)),
+            pltpu.SemaphoreType.DMA((2,)),
+            pltpu.SemaphoreType.DMA((2,)),
+            pltpu.SemaphoreType.DMA((2,)),
+            pltpu.SemaphoreType.DMA((3,)),
+            pltpu.SemaphoreType.DMA((2,)),
+            pltpu.SemaphoreType.DMA((2,)),
+            pltpu.SemaphoreType.DMA((8,)),
+            pltpu.SemaphoreType.DMA((9,)),
+        ],
+        compiler_params=pltpu.CompilerParams(
+            collective_id=0, has_side_effects=True, vmem_limit_bytes=40 * 2**20
+        ),
+    )(codes, features, weight, bias[None, :], cotangent, tile_values, rev_values)
+    return act, back, gw, gb[0]
 
 
 def solution(mesh):
@@ -117,8 +395,9 @@
         P("row", "rep", None, None),
         P("row", "rep"),
     )
+    pairs = mesh.shape["row"] == SLABS and mesh.shape["rep"] == 2
     return jax.shard_map(
-        local,
+        fused if pairs else general,
         mesh=mesh,
         in_specs=placed,
         out_specs=(P(("row", "rep"), None), P(("row", "rep"), None), P(), P()),

time: 382 us -> 89.9 us (0.24)
  waiting for transfers between devices: 119 us -> 0 us
  starting transfers between devices: 84.8 us -> 0 us
  Pallas kernels: 0 us -> 77 us
  blocking collectives: 56.7 us -> 0 us
  matrix products: 40.4 us -> 0 us
  other arithmetic: 35.9 us -> 2.3 us
  local copies, waits for them, and re-layouts: 28.9 us -> 9.53 us
  between operations: 15 us -> 0.67 us
    ppermute x16 -> x0, starting transfers between devices: 84.7 us -> none  [passed_along(): return lax.ppermute(value, axis, pairs)]
    psum x1 -> x0, waiting for transfers between devices: 82.9 us -> none  [local(): grad_weight, grad_bias = lax.psum((weight_term, bias_term), ('row', 'rep'))]
    pallas_call x0 -> x1, Pallas kernels: none -> 77 us  [fused(): pl.pallas_call(functools.partial(fused_kernel, scale), out_shape=(jax.Sha...]
    psum x3 -> x0, blocking collectives: 53.1 us -> none  [the longest x1 43.5 us: local(): grad_weight, grad_bias = lax.psum((weight_term, bias_term), ('row', 'rep'))]
    dot_general x35 -> x0, matrix products: 40.4 us -> none  [the longest x16 22.4 us: section_term(): jnp.einsum('tab,tbf->taf', tile_block, sources, preferred_element_type=jn...]
    ppermute x16 -> x0, waiting for transfers between devices: 36.6 us -> none  [passed_along(): return lax.ppermute(value, axis, pairs)]
    lt x16 -> x2, other arithmetic: 18.2 us -> 1.46 us  [codes_of(): slot < count[0][:, None]]
    gather x16 -> x0, local copies, waits for them, and re-layouts: 10.5 us -> none  [section_term(): sources = jnp.take(blocks, slot_index[:, 1], axis=0)]
  transfers between devices with their start and end apart: 17 -> 0, of which waited for: 15 -> 0; matrix products, arithmetic and copies ran while one was open for 17% -> 0% of each run, Pallas kernels for 0% -> 0%
where the time goes in v1:
time: 89.9 us; the launch traced here: 89.5 us
  Pallas kernels  77 us (86%)
  local copies, waits for them, and re-layouts  9.53 us (11%)
  other arithmetic  2.3 us (3%)
    pallas_call x1, Pallas kernels, fused(): pl.pallas_call(functools.partial(fused_kernel, scale), out_shape=(jax.Sha...  77 us
    unnamed x16, local copies, waits for them, and re-layouts  9.19 us

profile of v1, /device:TPU:0, one launch (start us, length us, event | category | flops | bytes accessed | tf_op | source)
XLA Modules:
  0.0 89.5 jit_solution(4659695390330211526)
XLA Ops:
  0.6 0.7 iota_compare_fusion.1
  1.4 0.1 lt.54
  1.4 0.7 iota_compare_fusion
  2.2 0.1 lt.59
  2.3 0.8 add_reduce_fusion
  3.1 0.1 add.31
  3.2 0.1 add.29
  3.3 0.0 copy-start
  3.3 1.6 %copy-done = bf16[1,8,8,128,128]{4,3,2,1,0:T(8,128)(2,1)S(1)} copy-done((bf16[1,8,8,128,128]{4,3,2,1,0:T(8,128)(2,1)S(1)}, bf16[1,8,8,128,128]{4,3,2,1,0:T(8,128)(2,1)}, u32[]{:S(2)}) %copy-start) | copy-done | bytes 2097176
  4.9 0.0 copy-start.1
  4.9 1.6 %copy-done.1 = bf16[1,8,8,128,128]{4,3,2,1,0:T(8,128)(2,1)S(1)} copy-done((bf16[1,8,8,128,128]{4,3,2,1,0:T(8,128)(2,1)S(1)}, bf16[1,8,8,128,128]{4,3,2,1,0:T(8,128)(2,1)}, u32[]{:S(2)}) %copy-start.1) | copy-done | bytes 2097176
  6.5 0.0 copy-start.2
  6.5 0.9 %copy-done.2 = bf16[512,256]{1,0:T(8,128)(2,1)S(1)} copy-done((bf16[512,256]{1,0:T(8,128)(2,1)S(1)}, bf16[512,256]{1,0:T(8,128)(2,1)}, u32[]{:S(2)}) %copy-start.2) | copy-done | bytes 262168
  7.4 0.0 copy-start.3
  7.4 0.9 %copy-done.3 = bf16[256,256]{1,0:T(8,128)(2,1)S(1)} copy-done((bf16[256,256]{1,0:T(8,128)(2,1)S(1)}, bf16[256,256]{1,0:T(8,128)(2,1)}, u32[]{:S(2)}) %copy-start.3) | copy-done | bytes 131096
  8.3 0.0 copy-start.4
  8.3 0.9 %copy-done.4 = bf16[256,256]{1,0:T(8,128)(2,1)S(1)} copy-done((bf16[256,256]{1,0:T(8,128)(2,1)S(1)}, bf16[256,256]{1,0:T(8,128)(2,1)}, u32[]{:S(2)}) %copy-start.4) | copy-done | bytes 131096
  9.2 0.0 copy-start.5
  9.2 0.7 copy-done.5
  9.9 77.0 %shard_map.129 = (bf16[256,256]{1,0:T(8,128)(2,1)S(1)}, bf16[256,256]{1,0:T(8,128)(2,1)S(1)}, f32[256,256]{1,0:T(8,128)S(1)}, f32[1,256]{1,0:T(1,128)S(1)}) custom-call(s32[8,128]{1,0:T(8,128)S(1)} %pad.4.codes_ref, bf16[512,256]{1,0:T(8,128)(2,1)S(1)} %copy-done.2, bf16[256,256]{1,0:T(8,128)(2,1)S(1)} %copy-done.3, f32[1,256]{1,0:T(1,128)S(1)} %bitcast.4, ...), custom_call_target="tpu_custom_call" | custom-call | tf_op jit(solution)/shard_map/pallas_call | solution.py:340
  87.0 0.7 copy.18
  87.6 0.7 copy.19
  88.3 0.7 copy.20
  89.0 0.6 copy.21
  (4 shorter events, 0.0 us)
Async XLA Ops:
  3.3 1.6 %copy-start = (bf16[1,8,8,128,128]{4,3,2,1,0:T(8,128)(2,1)S(1)}, bf16[1,8,8,128,128]{4,3,2,1,0:T(8,128)(2,1)}, u32[]{:S(2)}) copy-start(bf16[1,8,8,128,128]{4,3,2,1,0:T(8,128)(2,1)} %fwd_hbm.1) | copy-start | bytes 6291460
  4.9 1.6 %copy-start.1 = (bf16[1,8,8,128,128]{4,3,2,1,0:T(8,128)(2,1)S(1)}, bf16[1,8,8,128,128]{4,3,2,1,0:T(8,128)(2,1)}, u32[]{:S(2)}) copy-start(bf16[1,8,8,128,128]{4,3,2,1,0:T(8,128)(2,1)} %rev_hbm.1) | copy-start | bytes 6291460
  6.5 0.9 %copy-start.2 = (bf16[512,256]{1,0:T(8,128)(2,1)S(1)}, bf16[512,256]{1,0:T(8,128)(2,1)}, u32[]{:S(2)}) copy-start(bf16[512,256]{1,0:T(8,128)(2,1)} %feat_ref.1) | copy-start | bytes 786436
  7.4 0.9 %copy-start.3 = (bf16[256,256]{1,0:T(8,128)(2,1)S(1)}, bf16[256,256]{1,0:T(8,128)(2,1)}, u32[]{:S(2)}) copy-start(bf16[256,256]{1,0:T(8,128)(2,1)} %weight_ref.1) | copy-start | bytes 393220
  8.3 0.9 %copy-start.4 = (bf16[256,256]{1,0:T(8,128)(2,1)S(1)}, bf16[256,256]{1,0:T(8,128)(2,1)}, u32[]{:S(2)}) copy-start(bf16[256,256]{1,0:T(8,128)(2,1)} %cot_ref.1) | copy-start | bytes 393220
  9.2 0.7 copy-start.5

commit v2 on v1

--- a/solution.py
+++ b/solution.py
@@ -106,8 +106,9 @@
 
 def fused_kernel(
     scale,
-    codes_ref, feat_ref, weight_ref, bias_ref, cot_ref, fwd_hbm, rev_hbm,
+    codes_ref, feat_hbm, weight_hbm, bias_hbm, cot_hbm, fwd_hbm, rev_hbm,
     act_ref, back_ref, gw_ref, gb_ref,
+    weight_ref, bias_ref, cot_ref, load_sem,
     gathered, tiles, codes_all, codes_s, acc, peer_acc,
     mixed_v, gpre_v, term, term_in, part_p, in_p, part_q, in_q, part_z, final,
     send_sem, recv_sem, tile_own, tile_send, tile_recv, code_sem, acc_send, acc_recv, red_send, red_recv,
@@ -122,10 +123,17 @@
     twin, peer_p, peer_q = (me, other), (me + step_p, core), (me + step_q, core)
     plane = lax.rem(me, 4)
 
+    inner = lax.div(z * (3 - z), 2)
+    toward = 1 - 2 * lax.div(z, 2)
+
+    def level(k):
+        return z + toward * (k * (1 - inner) + inner * lax.div(k + 1, 2) * (2 * lax.rem(k, 2) - 1))
+
     def line(k):
-        return lax.rem(z + k, 4) * 4 + plane
-
-    peers_z = [(line(k), core) for k in (1, 2, 3)]
+        return level(k) * 4 + plane
+
+    peers_z = [(lax.rem(z + k, 4) * 4 + plane, core) for k in (1, 2, 3)]
+    above, below = (me + 4, core), (me - 4, core)
 
     def remote(src, dst, s, r, dev):
         return pltpu.make_async_remote_copy(
@@ -135,7 +143,22 @@
     barrier = pltpu.get_barrier_semaphore()
     for dev in [twin, peer_p, peer_q] + peers_z:
         pl.semaphore_signal(barrier, inc=1, device_id=dev, device_id_type=MESH)
-    gathered[0, me] = feat_ref[pl.ds(pl.multiple_of(core * HALF, HALF), HALF), :]
+    own_half = pl.ds(pl.multiple_of(core * HALF, HALF), HALF)
+    twin_half = pl.ds(pl.multiple_of(other * HALF, HALF), HALF)
+    loads = [
+        pltpu.make_async_copy(src, dst, load_sem.at[i])
+        for i, (src, dst) in enumerate(
+            [
+                (feat_hbm.at[own_half], gathered.at[0, me]),
+                (weight_hbm, weight_ref),
+                (bias_hbm, bias_ref),
+                (cot_hbm, cot_ref),
+            ]
+        )
+    ]
+    for load in loads:
+        load.start()
+    loads[0].wait()
     pl.semaphore_wait(barrier, 6)
 
     def piece(phase, slab, sem, dev):
@@ -145,19 +168,34 @@
         )
 
     def send_own(phase):
-        for k, dev in enumerate(peers_z):
-            piece(phase, me, k, dev).start()
-        piece(phase, me, 3, peer_p).start()
-        piece(phase, me, 7, peer_q).start()
-
-    def forward_line(phase):
+        @pl.when(z < 3)
+        def _():
+            piece(phase, me, 12 + z, above).start()
+
+        @pl.when(z > 0)
+        def _():
+            piece(phase, me, 16 + z, below).start()
+
+        piece(phase, me, 0, peer_p).start()
+        piece(phase, me, 4, peer_q).start()
+
+    def forward_line(phase, first, last):
         def body(k, carry):
-            slab = line(k)
+            at, slab = level(k), line(k)
             piece(phase, slab, 0, peer_p).wait_recv()
-            piece(phase, slab, 3 + k, peer_p).start()
-            piece(phase, slab, 7 + k, peer_q).start()
+
+            @pl.when((at < z) & (z < 3))
+            def _():
+                piece(phase, slab, 12 + at, above).start()
+
+            @pl.when((at > z) & (z > 0))
+            def _():
+                piece(phase, slab, 16 + at, below).start()
+
+            piece(phase, slab, k, peer_p).start()
+            piece(phase, slab, 4 + k, peer_q).start()
             return carry
-        lax.fori_loop(1, 4, body, 0)
+        lax.fori_loop(first, last, body, 0)
 
     def term_of(phase, slab):
         offset = lax.rem(slab - me + SLABS, SLABS)
@@ -182,14 +220,14 @@
                 jnp.concatenate(lefts[n], axis=1), right, preferred_element_type=jnp.float32
             )
 
-    def forward_p(phase):
+    def forward_p(phase, first, last):
         def body(k, carry):
             slab = line(k) + step_p
             piece(phase, slab, 0, peer_q).wait_recv()
-            piece(phase, slab, 11 + k, peer_q).start()
+            piece(phase, slab, 8 + k, peer_q).start()
             term_of(phase, line(k))
             return carry
-        lax.fori_loop(0, 4, body, 0)
+        lax.fori_loop(first, last, body, 0)
 
     def add_p(phase):
         def body(k, carry):
@@ -204,9 +242,6 @@
             term_of(phase, slab)
             return carry
         lax.fori_loop(first, last, body, 0)
-
-    own_half = pl.ds(pl.multiple_of(core * HALF, HALF), HALF)
-    twin_half = pl.ds(pl.multiple_of(other * HALF, HALF), HALF)
 
     def swap_acc(phase):
         copy = remote(
@@ -231,7 +266,7 @@
     near.start()
     far.start()
     acc[...] = jnp.zeros_like(acc)
-    forward_line(0)
+    forward_line(0, 1, 4)
     code_copy.wait()
     to_scalar = pltpu.make_async_copy(codes_all, codes_s, code_sem.at[2])
     to_scalar.start()
@@ -241,10 +276,12 @@
     near, far = tile_copies(1, rev_hbm)
     near.start()
     far.start()
-    forward_p(0)
+    forward_p(0, 0, 4)
     add_p(0)
     add_q(0, 0, 8)
 
+    for load in loads[1:]:
+        load.wait()
     mixed = swap_acc(0).astype(jnp.bfloat16)
     mixed_v[...] = mixed
     preact = jnp.dot(mixed, weight_ref[...], preferred_element_type=jnp.float32) + bias_ref[...]
@@ -268,7 +305,6 @@
         term[h, 72:136, :] = whole[128 * h + 64:128 * h + 128]
     to_twin = remote(term.at[other], term_in, red_send.at[0], red_recv.at[0], twin)
     to_twin.start()
-    forward_line(1)
     near.wait()
     far.wait()
     to_twin.wait()
@@ -277,12 +313,12 @@
     give = pl.ds(pl.multiple_of((1 - bit_p) * 64, 8), PART)
     to_p = remote(part_p.at[give], in_p, red_send.at[1], red_recv.at[1], peer_p)
     to_p.start()
-    forward_p(1)
+    forward_line(1, 1, 2)
     to_p.wait()
     part_q[...] = part_p[keep, :] + in_p[...]
     to_q = remote(part_q, in_q, red_send.at[2], red_recv.at[2], peer_q)
     to_q.start()
-    add_p(1)
+    forward_line(1, 2, 4)
     to_q.wait()
     part_z[z] = part_q[...] + in_q[...]
     to_z = [
@@ -291,7 +327,7 @@
     ]
     for copy in to_z:
         copy.start()
-    add_q(1, 0, 4)
+    forward_p(1, 0, 4)
     for k in (1, 2, 3):
         at = lax.rem(z + k, 4)
         remote(part_z.at[at], part_z.at[at], red_send.at[3], red_recv.at[3 + at], twin).wait_recv()
@@ -299,11 +335,12 @@
     up = final.at[core, pl.ds(pl.multiple_of(bit_p * PART, 8), 64)]
     up_p = remote(up, up, red_send.at[6], red_recv.at[7], peer_p)
     up_p.start()
-    add_q(1, 4, 6)
+    add_p(1)
+    add_q(1, 0, 4)
     up_p.wait()
     up_twin = remote(final.at[core], final.at[core], red_send.at[7], red_recv.at[8], twin)
     up_twin.start()
-    add_q(1, 6, 8)
+    add_q(1, 4, 8)
     copy = remote(acc.at[1, twin_half], peer_acc.at[1], acc_send.at[1], acc_recv.at[1], twin)
     copy.start()
     up_twin.wait()
@@ -319,7 +356,15 @@
         def drain(k, carry):
             piece(phase, me, k, twin).wait_send()
             return carry
-        lax.fori_loop(0, 15, drain, 0)
+        lax.fori_loop(0, 12, drain, 0)
+        for at in range(4):
+            @pl.when((z < 3) & (at <= z))
+            def _():
+                piece(phase, me, 12 + at, twin).wait_send()
+
+            @pl.when((z > 0) & (at >= z))
+            def _():
+                piece(phase, me, 16 + at, twin).wait_send()
 
 
 def codes_of(index, count):
@@ -345,9 +390,13 @@
             jax.ShapeDtypeStruct((WIDTH, WIDTH), f32),
             jax.ShapeDtypeStruct((1, WIDTH), f32),
         ),
-        in_specs=[vmem] * 5 + [anywhere] * 2,
+        in_specs=[vmem] + [anywhere] * 6,
         out_specs=(vmem,) * 4,
         scratch_shapes=[
+            pltpu.VMEM((WIDTH, WIDTH), bf16),
+            pltpu.VMEM((1, WIDTH), f32),
+            pltpu.VMEM((HALF, WIDTH), bf16),
+            pltpu.SemaphoreType.DMA((4,)),
             pltpu.VMEM((2, SLABS, HALF, WIDTH), bf16),
             pltpu.VMEM((2, SLABS, SLOTS, TILE, TILE), bf16),
             pltpu.VMEM((2, 8, 128), jnp.int32),
@@ -364,7 +413,7 @@
             pltpu.VMEM((PART, WIDTH), f32),
             pltpu.VMEM((4, PART, WIDTH), f32),
             pltpu.VMEM((2, BLOCK, WIDTH), f32),
-            pltpu.SemaphoreType.DMA((2, 15)),
+            pltpu.SemaphoreType.DMA((2, 20)),
             pltpu.SemaphoreType.DMA((2, SLABS)),
             pltpu.SemaphoreType.DMA((2,)),
             pltpu.SemaphoreType.DMA((2,)),
@@ -376,7 +425,7 @@
             pltpu.SemaphoreType.DMA((9,)),
         ],
         compiler_params=pltpu.CompilerParams(
-            collective_id=0, has_side_effects=True, vmem_limit_bytes=40 * 2**20
+            collective_id=0, has_side_effects=True, vmem_limit_bytes=60 * 2**20
         ),
     )(codes, features, weight, bias[None, :], cotangent, tile_values, rev_values)
     return act, back, gw, gb[0]

time: 89.9 us -> 72.8 us (0.81)
  Pallas kernels: 77 us -> 62.6 us
  local copies, waits for them, and re-layouts: 9.53 us -> 6.99 us
    pallas_call x1, Pallas kernels: 77 us -> 62.6 us  [fused(): pl.pallas_call(functools.partial(fused_kernel, scale), out_shape=(jax.Sha...]
    unnamed x16 -> x4, local copies, waits for them, and re-layouts: 9.19 us -> 6.05 us
where the time goes in v2:
time: 72.8 us; the launch traced here: 72.5 us
  Pallas kernels  62.6 us (86%)
  local copies, waits for them, and re-layouts  6.99 us (10%)
  other arithmetic  2.3 us (3%)
    pallas_call x1, Pallas kernels, fused(): pl.pallas_call(functools.partial(fused_kernel, scale), out_shape=(jax.Sha...  62.6 us
    unnamed x4, local copies, waits for them, and re-layouts  6.05 us
    lt x2, other arithmetic, codes_of(): slot < count[0][:, None]  1.46 us

profile of v2, /device:TPU:0, one launch (start us, length us, event | category | flops | bytes accessed | tf_op | source)
XLA Modules:
  0.0 72.5 jit_solution(12614320947724546204)
XLA Ops:
  0.6 0.7 %iota_compare_fusion.1 = pred[8,8]{1,0:T(8,128)(4,1)S(1)} fusion(s32[8]{0:T(128)} %bitcast.6), kind=kLoop, calls=%fused_computation.3 | loop fusion | flops 64 | bytes 96 | tf_op jit(solution)/shard_map/lt | solution.py:373
  1.4 0.1 lt.54
  1.4 0.7 %iota_compare_fusion = pred[8,8]{1,0:T(8,128)(4,1)S(1)} fusion(s32[8]{0:T(128)} %bitcast.7), kind=kLoop, calls=%fused_computation.1 | loop fusion | flops 64 | bytes 96 | tf_op jit(solution)/shard_map/lt | solution.py:373
  2.2 0.1 lt.59
  2.3 0.8 %add_reduce_fusion = (s32[8,8]{1,0:T(8,128)S(1)}, s32[8,8]{1,0:T(8,128)S(1)}) fusion(s32[1,8,8,2]{2,3,1,0:T(2,128)} %param.18, s32[1,8,8,2]{2,3,1,0:T(2,128)} %param.15), kind=kLoop, calls=%fused_computation | loop fusion | flops 256 | bytes 1536 | tf_op jit(solution)/shard_map/add | solution.py:372
  3.1 0.1 add.31
  3.2 0.1 add.29
  3.3 0.6 pad.4.codes_ref
  3.9 62.6 %shard_map.129 = (bf16[256,256]{1,0:T(8,128)(2,1)}, bf16[256,256]{1,0:T(8,128)(2,1)}, f32[256,256]{1,0:T(8,128)}, f32[1,256]{1,0:T(1,128)}) custom-call(s32[8,128]{1,0:T(8,128)} %pad.4.codes_ref, bf16[512,256]{1,0:T(8,128)(2,1)} %feat_hbm.1, bf16[256,256]{1,0:T(8,128)(2,1)} %weight_hbm.1, f32[1,256]{1,0:T(1,128)} %bitcast.4, bf16[256,256]{1,0:T(8,128)(2,1)} %cot_hbm.1, ...), custom_call_target="tpu_custom_call" | custom-call | tf_op jit(solution)/shard_map/pallas_call | solution.py:385
  66.4 1.6 %copy.18 = bf16[256,256]{1,0:T(8,128)(2,1)} copy(bf16[256,256]{1,0:T(8,128)(2,1)} %get-tuple-element.18) | data formatting | bytes 262144
  68.0 1.6 %copy.19 = bf16[256,256]{1,0:T(8,128)(2,1)} copy(bf16[256,256]{1,0:T(8,128)(2,1)} %get-tuple-element.19) | data formatting | bytes 262144
  69.6 1.7 %copy.20 = f32[256,256]{1,0:T(8,128)} copy(f32[256,256]{1,0:T(8,128)} %get-tuple-element.20) | data formatting | bytes 524288
  71.3 1.2 %copy.21 = f32[256]{0:T(256)} copy(f32[256]{0:T(256)} %bitcast.5) | data formatting | bytes 2048
  (3 shorter events, 0.0 us)
